TPU v7x, 128 devices: a whole 4x4x4 slice. The times are simulated.
128 devices in a mesh: seq: 16 (over z, x_lo, core), head: 8 (over y, x_hi).
Axes of the slice: x: 4 (x_hi: 2, x_lo: 2; x = x_hi * 2 + x_lo), y: 4, z: 4, core: 2. Of those that a mesh axis runs over, the one named last changes fastest.
Arguments:
- teacher: bfloat16 [2048, 3, 8192], P('seq', None, 'head')
- student: bfloat16 [2048, 3, 4096], P('seq', None, 'head')
- table: int32 [64], replicated, may hold values from 0 to 63, each once
Outputs:
- loss: float32 [], replicated
- grads: bfloat16 [2048, 3, 4096], P('seq', None, 'head')
Inputs may be any that keep to these rules, and one draw needn't show every extreme that they name: `table`: each teacher head stands in exactly one slot.
All inputs are finite; a program needn't handle non-finite values.
Results may differ from a plain program's by a relative error of at most 0.0055.
Values may be sent and summed in bfloat16 or wider, within the bound.
A program may use at most 128 MiB of HBM per device.

v0:
```python
import math

import jax
import jax.numpy as jnp
from jax import lax
from jax.sharding import PartitionSpec as P

HD = 128
GRP = 2


NEG_FILL = -1e30


def body(teacher, student, table):
    rows_here = teacher.shape[0]
    seq_count = lax.axis_size("seq")
    seq_rank = lax.axis_index("seq")
    head_rank = lax.axis_index("head")
    teach_width = teacher.shape[2]
    stud_width = student.shape[2]
    slots_here = teach_width // HD
    rel_here = stud_width // HD
    total_rows = rows_here * seq_count
    key_span = math.gcd(total_rows, 512)
    block_count = total_rows // key_span
    scale_teach = 1.0 / math.sqrt(GRP * HD)
    scale_stud = 1.0 / math.sqrt(HD)
    wanted = lax.dynamic_slice_in_dim(table, head_rank * slots_here, slots_here)
    shard_part = lax.all_gather(teacher, "head", axis=2, tiled=True)
    held = shard_part.shape[2] // HD
    blocks = shard_part.reshape(rows_here, 3, held, HD)
    numbers = jnp.arange(held, dtype=jnp.int32)
    onehot = (wanted[:, None] == numbers[None, :]).astype(jnp.bfloat16)
    chosen = jnp.einsum("tahd,sh->tasd", blocks, onehot, preferred_element_type=jnp.float32)
    own_teach = chosen.astype(jnp.bfloat16).reshape(rows_here, 3, teach_width)
    all_teach, all_stud = (
        lax.all_gather(own_teach, "seq", axis=0, tiled=True),
        lax.all_gather(student, "seq", axis=0, tiled=True),
    )
    query_teach = own_teach.reshape(rows_here, 3, rel_here, GRP * HD)
    query_stud = student.reshape(rows_here, 3, rel_here, HD)
    first_own = seq_rank * rows_here
    positions = first_own + jnp.arange(rows_here, dtype=jnp.int32)

    def logits(first_key, span_rows):
        key_teach = lax.dynamic_slice_in_dim(all_teach, first_key, span_rows, 0).reshape(
            span_rows, 3, rel_here, GRP * HD
        )
        key_stud = lax.dynamic_slice_in_dim(all_stud, first_key, span_rows, 0).reshape(
            span_rows, 3, rel_here, HD
        )
        teach_logit = (
            jnp.einsum(
                "qahd,kahd->ahqk", query_teach, key_teach, preferred_element_type=jnp.float32
            )
            * scale_teach
        )
        stud_logit = (
            jnp.einsum("qahd,kahd->ahqk", query_stud, key_stud, preferred_element_type=jnp.float32)
            * scale_stud
        )
        allowed = (first_key + jnp.arange(span_rows, dtype=jnp.int32))[None, :] <= positions[
            :, None
        ]
        return (
            jnp.where(allowed, teach_logit, NEG_FILL),
            jnp.where(allowed, stud_logit, NEG_FILL),
            allowed,
            key_stud,
        )

    def forward_step(block_index, carried):
        max_teach, sum_teach, cross, max_stud, sum_stud = carried
        teach_logit, stud_logit, allowed, key_stud = logits(block_index * key_span, key_span)
        new_teach = jnp.maximum(max_teach, jnp.max(teach_logit, axis=-1))
        weights = jnp.exp(teach_logit - new_teach[..., None])
        factor = jnp.exp(max_teach - new_teach)
        sum_teach = sum_teach * factor + jnp.sum(weights, axis=-1)
        cross = cross * factor + jnp.sum(
            weights * jnp.where(allowed, teach_logit - stud_logit, 0.0), axis=-1
        )
        new_stud = jnp.maximum(max_stud, jnp.max(stud_logit, axis=-1))
        sum_stud = sum_stud * jnp.exp(max_stud - new_stud) + jnp.sum(
            jnp.exp(stud_logit - new_stud[..., None]), axis=-1
        )
        return (new_teach, sum_teach, cross, new_stud, sum_stud)

    stat_shape = (3, rel_here, rows_here)
    lowest = jnp.full(stat_shape, NEG_FILL, jnp.float32)
    nothing = jnp.zeros(stat_shape, jnp.float32)
    max_teach, sum_teach, cross, max_stud, sum_stud = lax.fori_loop(
        0, block_count, forward_step, (lowest, nothing, nothing, lowest, nothing)
    )
    lse_teach = max_teach + jnp.log(sum_teach)
    lse_stud = max_stud + jnp.log(sum_stud)
    kl_rows = cross / sum_teach - lse_teach + lse_stud
    kl_total = lax.psum(jnp.sum(kl_rows), ("seq", "head"))
    loss = kl_total / (3.0 * rel_here * lax.axis_size("head") * total_rows)

    def gradient_tile(first_key, span_rows):
        teach_logit, stud_logit, allowed, key_stud = logits(first_key, span_rows)
        diff = jnp.exp(stud_logit - lse_stud[..., None]) - jnp.exp(
            teach_logit - lse_teach[..., None]
        )
        return (diff.astype(jnp.bfloat16), key_stud)

    def backward_step(block_index, carried):
        row_grad, col_grad = carried
        first_key = block_index * key_span
        diff, key_stud = gradient_tile(first_key, key_span)
        row_grad = row_grad + jnp.einsum(
            "ahqk,kahd->qahd", diff, key_stud, preferred_element_type=jnp.float32
        )
        return (row_grad, col_grad)

    col_rows = 1
    start_row = jnp.zeros((rows_here, 3, rel_here, HD), jnp.float32)
    start_col = jnp.zeros((col_rows, 3, stud_width), jnp.float32)
    row_grad, col_grad = lax.fori_loop(0, block_count, backward_step, (start_row, start_col))
    all_stats = lax.all_gather(jnp.stack([lse_teach, lse_stud], 0), "seq", axis=3, tiled=True)

    def owner_step(block_index, running):
        first_query = block_index * key_span
        span_teach = lax.dynamic_slice_in_dim(all_teach, first_query, key_span, 0).reshape(
            key_span, 3, rel_here, GRP * HD
        )
        span_stud = lax.dynamic_slice_in_dim(all_stud, first_query, key_span, 0).reshape(
            key_span, 3, rel_here, HD
        )
        span_stats = lax.dynamic_slice_in_dim(all_stats, first_query, key_span, 3)
        teach_logit = (
            jnp.einsum(
                "qahd,kahd->ahqk", span_teach, query_teach, preferred_element_type=jnp.float32
            )
            * scale_teach
        )
        stud_logit = (
            jnp.einsum("qahd,kahd->ahqk", span_stud, query_stud, preferred_element_type=jnp.float32)
            * scale_stud
        )
        query_pos = first_query + jnp.arange(key_span, dtype=jnp.int32)
        allowed = positions[None, :] <= query_pos[:, None]
        teach_logit = jnp.where(allowed, teach_logit, NEG_FILL)
        stud_logit = jnp.where(allowed, stud_logit, NEG_FILL)
        diff = jnp.exp(stud_logit - span_stats[1][..., None]) - jnp.exp(
            teach_logit - span_stats[0][..., None]
        )
        diff = diff.astype(jnp.bfloat16)
        return running + jnp.einsum(
            "ahqk,qahd->kahd", diff, span_stud, preferred_element_type=jnp.float32
        )

    col_own = lax.fori_loop(
        0, block_count, owner_step, jnp.zeros((rows_here, 3, rel_here, HD), jnp.float32)
    )
    col_sum = col_own.reshape(rows_here, 3, stud_width)
    grads = ((row_grad.reshape(rows_here, 3, stud_width) + col_sum) * scale_stud).astype(
        jnp.bfloat16
    )
    return (loss, grads)


def solution(mesh):
    return jax.shard_map(
        body,
        mesh=mesh,
        in_specs=(P("seq", None, "head"), P("seq", None, "head"), P()),
        out_specs=(P(), P("seq", None, "head")),
        check_vma=False,
    )
```

profile of v0, /device:TPU:1, one launch (start us, length us, event | category | flops | bytes accessed | tf_op | source)
XLA Modules:
  0.0 472.4 jit_solution(13872625156213432405)
XLA Ops:
  7.2 2.3 copy.14
  11.7 90.3 %all-gather.4.cloned.1.call-done = bf16[128,3,8192]{0,2,1:T(8,128)(2,1)} async-done(((bf16[128,3,1024]{0,2,1:T(8,128)(2,1)}), bf16[128,3,8192]{0,2,1:T(8,128)(2,1)}) %all-gather.4.cloned.1.call-update) | async-done | bytes 6291472 | tf_op jit(solution)/shard_map/all_gather | solution.py:30
  102.0 9.1 %copy.15 = bf16[128,3,64,128]{3,2,1,0:T(8,128)(2,1)} copy(bf16[128,3,64,128]{0,3,2,1:T(8,128)(2,1)} %bitcast.138) | data formatting | bytes 12582912 | tf_op jit(solution)/shard_map/reshape | solution.py:32
  111.1 4.1 fusion.34
  117.8 38.3 %all-gather.8.cloned.1.call-done = bf16[2048,3,512]{0,2,1:T(8,128)(2,1)} async-done(((bf16[128,3,512]{0,2,1:T(8,128)(2,1)}), bf16[2048,3,512]{0,2,1:T(8,128)(2,1)}) %all-gather.8.cloned.1.call-update) | async-done | bytes 6291472 | tf_op jit(solution)/shard_map/all_gather | solution.py:39
  156.1 80.4 %all-gather.6.cloned.1.call-done = bf16[2048,3,1024]{0,2,1:T(8,128)(2,1)} async-done(((bf16[128,3,1024]{0,2,1:T(8,128)(2,1)}), bf16[2048,3,1024]{0,2,1:T(8,128)(2,1)}) %all-gather.6.cloned.1.call-update) | async-done | bytes 12582928 | tf_op jit(solution)/shard_map/all_gather | solution.py:38
  236.5 32.0 %while.50 = (s32[]{:T(128)}, f32[3,4,128]{2,1,0:T(4,128)S(1)}, f32[3,4,128]{2,1,0:T(4,128)S(1)}, f32[3,4,128]{2,1,0:T(4,128)S(1)}, f32[3,4,128]{2,1,0:T(4,128)S(...) while((s32[]{:T(128)}, f32[3,4,128]{2,1,0:T(4,128)S(1)}, ...), condition=%wide.region_6.7_spmd.clone, body=%wide.region_0.6_spmd.clone.sunk | while | flops 618220160 | bytes 31450332 | solution.py:92
  269.1 64.8 %psum.7 = f32[]{:T(128)} all-reduce(f32[]{:T(128)} %get-tuple-element.692), channel_id=1, replica_groups=mesh['seq'=16,'head'=8] {'seq','head'}, use_global_device_ids=true, to_apply=%region_8.9 | all-reduce | flops 1 | bytes 8 | tf_op jit(solution)/shard_map/psum | solution.py:98
  333.9 18.8 %all_gather.15 = f32[2,3,4,2048]{3,2,1,0:T(4,128)S(1)} all-gather(f32[2,3,4,128]{3,2,1,0:T(4,128)S(1)} %pad_maximum_fusion), channel_id=1, replica_groups=mesh['seq'=16,'head'=8] {'seq'}, dimensions={3}, use_global_device_ids=true | all-gather | bytes 208896 | tf_op jit(solution)/shard_map/all_gather | solution.py:121
  352.7 54.2 %while.52 = (s32[]{:T(128)}, f32[128,3,4,128]{0,3,2,1:T(8,128)}, bf16[2048,3,512]{0,2,1:T(8,128)(2,1)}, bf16[128,3,4,128]{3,2,1,0:T(4,128)(2,1)S(1)}, f32[2,3,4,...) while((s32[]{:T(128)}, f32[128,3,4,128]{0,3,2,1:T(8,128)}, ...), condition=%wide.region_12.13_spmd.clone, body=%wide.region_11.12_spmd.clone.sunk | while | flops 812057216 | bytes 25056480 | solution.py:154
  354.4 3.8 constant_dynamic-slice_fusion.17
  358.1 2.3 fusion.90
  360.5 5.7 %fusion.91 = f32[128,3,4,128]{0,3,2,1:T(8,128)} fusion(bf16[512,3,4,128]{0,3,2,1:T(8,128)(2,1)S(1)} %bitcast.135, f32[3,4,512,128]{3,2,1,0:T(8,128)} %fusion.90, bf16[512,3,4,256]{0,3,2,1:T(8,128)(2,1)} %bitcast.136, f32[3,4,512]{2,1,0:T(4,128)S(1)} %get-tuple-element.892, f32[3,4,512]{2,1,0:T(4,128)S(1)} %get-tuple-element.893, ...), kind=kOutput, calls=%fused_computation.48.clone.1 | convolution fusion | flops 610664448 | bytes 10338305 | tf_op jit(solution)/shard_map/while/body/eval_jaxpr/ahqk,qahd->kahd/dot_general | solution.py:150
  367.9 3.8 constant_dynamic-slice_fusion.17
  371.7 2.3 fusion.90
  374.0 5.8 %fusion.91 = f32[128,3,4,128]{0,3,2,1:T(8,128)} fusion(bf16[512,3,4,128]{0,3,2,1:T(8,128)(2,1)S(1)} %bitcast.135, f32[3,4,512,128]{3,2,1,0:T(8,128)} %fusion.90, bf16[512,3,4,256]{0,3,2,1:T(8,128)(2,1)} %bitcast.136, f32[3,4,512]{2,1,0:T(4,128)S(1)} %get-tuple-element.892, f32[3,4,512]{2,1,0:T(4,128)S(1)} %get-tuple-element.893, ...), kind=kOutput, calls=%fused_computation.48.clone.1 | convolution fusion | flops 610664448 | bytes 10338305 | tf_op jit(solution)/shard_map/while/body/eval_jaxpr/ahqk,qahd->kahd/dot_general | solution.py:150
  381.5 3.8 constant_dynamic-slice_fusion.17
  385.2 2.3 fusion.90
  387.6 5.8 %fusion.91 = f32[128,3,4,128]{0,3,2,1:T(8,128)} fusion(bf16[512,3,4,128]{0,3,2,1:T(8,128)(2,1)S(1)} %bitcast.135, f32[3,4,512,128]{3,2,1,0:T(8,128)} %fusion.90, bf16[512,3,4,256]{0,3,2,1:T(8,128)(2,1)} %bitcast.136, f32[3,4,512]{2,1,0:T(4,128)S(1)} %get-tuple-element.892, f32[3,4,512]{2,1,0:T(4,128)S(1)} %get-tuple-element.893, ...), kind=kOutput, calls=%fused_computation.48.clone.1 | convolution fusion | flops 610664448 | bytes 10338305 | tf_op jit(solution)/shard_map/while/body/eval_jaxpr/ahqk,qahd->kahd/dot_general | solution.py:150
  395.1 3.8 constant_dynamic-slice_fusion.17
  398.8 2.3 fusion.90
  401.1 5.8 %fusion.91 = f32[128,3,4,128]{0,3,2,1:T(8,128)} fusion(bf16[512,3,4,128]{0,3,2,1:T(8,128)(2,1)S(1)} %bitcast.135, f32[3,4,512,128]{3,2,1,0:T(8,128)} %fusion.90, bf16[512,3,4,256]{0,3,2,1:T(8,128)(2,1)} %bitcast.136, f32[3,4,512]{2,1,0:T(4,128)S(1)} %get-tuple-element.892, f32[3,4,512]{2,1,0:T(4,128)S(1)} %get-tuple-element.893, ...), kind=kOutput, calls=%fused_computation.48.clone.1 | convolution fusion | flops 610664448 | bytes 10338305 | tf_op jit(solution)/shard_map/while/body/eval_jaxpr/ahqk,qahd->kahd/dot_general | solution.py:150
  406.9 54.8 %while.51 = (s32[]{:T(128)}, f32[128,3,4,128]{0,3,2,1:T(8,128)}, bf16[2048,3,512]{0,2,1:T(8,128)(2,1)}, bf16[128,3,4,128]{3,2,1,0:T(4,128)(2,1)S(1)}, f32[3,4,12...) while((s32[]{:T(128)}, f32[128,3,4,128]{0,3,2,1:T(8,128)}, ...), condition=%wide.region_10.11_spmd.clone, body=%wide.region_9.10_spmd.clone.sunk | while | flops 812057216 | bytes 24921292 | solution.py:120
  408.6 3.8 constant_dynamic-slice_fusion.15
  412.3 2.2 fusion.83
  414.6 5.9 %fusion.84 = f32[128,3,4,128]{0,3,2,1:T(8,128)} fusion(bf16[512,3,4,128]{0,3,2,1:T(8,128)(2,1)S(1)} %bitcast.132, f32[3,4,512,128]{2,3,1,0:T(8,128)} %fusion.83, bf16[512,3,4,256]{0,3,2,1:T(8,128)(2,1)} %bitcast.137, f32[3,4,128]{2,1,0:T(4,128)S(1)} %get-tuple-element.972, f32[3,4,128]{2,1,0:T(4,128)S(1)} %get-tuple-element.969, ...), kind=kOutput, calls=%fused_computation.34.clone.1 | convolution fusion | flops 610664448 | bytes 10301441 | tf_op jit(solution)/shard_map/while/body/eval_jaxpr/ahqk,kahd->qahd/dot_general | solution.py:112
  422.2 3.8 constant_dynamic-slice_fusion.15
  428.2 6.1 %fusion.84 = f32[128,3,4,128]{0,3,2,1:T(8,128)} fusion(bf16[512,3,4,128]{0,3,2,1:T(8,128)(2,1)S(1)} %bitcast.132, f32[3,4,512,128]{2,3,1,0:T(8,128)} %fusion.83, bf16[512,3,4,256]{0,3,2,1:T(8,128)(2,1)} %bitcast.137, f32[3,4,128]{2,1,0:T(4,128)S(1)} %get-tuple-element.972, f32[3,4,128]{2,1,0:T(4,128)S(1)} %get-tuple-element.969, ...), kind=kOutput, calls=%fused_computation.34.clone.1 | convolution fusion | flops 610664448 | bytes 10301441 | tf_op jit(solution)/shard_map/while/body/eval_jaxpr/ahqk,kahd->qahd/dot_general | solution.py:112
  435.9 3.8 constant_dynamic-slice_fusion.15
  441.9 6.1 %fusion.84 = f32[128,3,4,128]{0,3,2,1:T(8,128)} fusion(bf16[512,3,4,128]{0,3,2,1:T(8,128)(2,1)S(1)} %bitcast.132, f32[3,4,512,128]{2,3,1,0:T(8,128)} %fusion.83, bf16[512,3,4,256]{0,3,2,1:T(8,128)(2,1)} %bitcast.137, f32[3,4,128]{2,1,0:T(4,128)S(1)} %get-tuple-element.972, f32[3,4,128]{2,1,0:T(4,128)S(1)} %get-tuple-element.969, ...), kind=kOutput, calls=%fused_computation.34.clone.1 | convolution fusion | flops 610664448 | bytes 10301441 | tf_op jit(solution)/shard_map/while/body/eval_jaxpr/ahqk,kahd->qahd/dot_general | solution.py:112
  449.6 3.8 constant_dynamic-slice_fusion.15
  455.6 6.1 %fusion.84 = f32[128,3,4,128]{0,3,2,1:T(8,128)} fusion(bf16[512,3,4,128]{0,3,2,1:T(8,128)(2,1)S(1)} %bitcast.132, f32[3,4,512,128]{2,3,1,0:T(8,128)} %fusion.83, bf16[512,3,4,256]{0,3,2,1:T(8,128)(2,1)} %bitcast.137, f32[3,4,128]{2,1,0:T(4,128)S(1)} %get-tuple-element.972, f32[3,4,128]{2,1,0:T(4,128)S(1)} %get-tuple-element.969, ...), kind=kOutput, calls=%fused_computation.34.clone.1 | convolution fusion | flops 610664448 | bytes 10301441 | tf_op jit(solution)/shard_map/while/body/eval_jaxpr/ahqk,kahd->qahd/dot_general | solution.py:112
  (119 shorter events, 59.2 us)
Async XLA Ops:
  7.2 4.4 copy-start.1
  7.2 94.8 %all-gather.4.cloned.1.call-start = ((), (), s32[]{:S(2)}) async-start(), calls=%async_computation | async-start | bytes 7077888 | tf_op jit(solution)/shard_map/all_gather | solution.py:30
  9.5 146.6 %all-gather.8.cloned.1.call-start = ((), (), s32[]{:S(2)}) async-start(), calls=%async_computation.2 | async-start | bytes 6684672 | tf_op jit(solution)/shard_map/all_gather | solution.py:39
  11.5 224.9 %all-gather.6.cloned.1.call-start = ((), (), s32[]{:S(2)}) async-start(), calls=%async_computation.1 | async-start | bytes 13369344 | tf_op jit(solution)/shard_map/all_gather | solution.py:38
  111.1 5.5 %copy-start = (bf16[128,3,512]{0,2,1:T(8,128)(2,1)S(1)}, bf16[128,3,512]{0,2,1:T(8,128)(2,1)}, u32[]{:S(2)}) copy-start(bf16[128,3,512]{0,2,1:T(8,128)(2,1)} %copy.17) | copy-start | bytes 1179652
Sparse Core Ops, SparseCore 0:
  10.3 91.6 all-gather.3
  104.2 51.8 all-gather.7
  157.7 78.7 all-gather.5
where the time goes:
time: 474 us; the launch traced here: 472 us
  waiting for transfers between devices  209 us (44%)
  blocking collectives  83.6 us (18%)
  matrix products  79 us (17%)
  local copies, waits for them, and re-layouts  73.5 us (16%)
  between operations  15.7 us (3%)
  other arithmetic  11 us (2%)
    all_gather x1, waiting for transfers between devices, body(): shard_part = lax.all_gather(teacher, 'head', axis=2, tiled=True)  90.3 us
    all_gather x1, waiting for transfers between devices, body(): lax.all_gather(own_teach, 'seq', axis=0, tiled=True)  80.4 us
    psum x1, blocking collectives, body(): kl_total = lax.psum(jnp.sum(kl_rows), ('seq', 'head'))  64.8 us
    all_gather x1, waiting for transfers between devices, body(): lax.all_gather(student, 'seq', axis=0, tiled=True)  38.3 us
    dot_general x4, matrix products, backward_step(): jnp.einsum('ahqk,kahd->qahd', diff, key_stud, preferred_element_type=jnp....  24.2 us
    dynamic_slice x8, local copies, waits for them, and re-layouts, logits(): lax.dynamic_slice_in_dim(all_teach, first_key, span_rows, 0)  23.4 us
    dot_general x4, matrix products, owner_step(): jnp.einsum('ahqk,qahd->kahd', diff, span_stud, preferred_element_type=jnp...  23.2 us
    all_gather x1, blocking collectives, body(): lax.all_gather(jnp.stack([lse_teach, lse_stud], 0), 'seq', axis=3, tiled=...  18.8 us
  transfers between devices with their start and end apart: 3, of which 3 were waited for; matrix products, arithmetic and copies ran while one was open for 4% of the time, Pallas kernels for 0%

commit v1 on v0

v1 whole, which is shorter than its diff:
```python
import functools
import math

import jax
import jax.numpy as jnp
from jax import lax
from jax.experimental import pallas as pl
from jax.experimental.pallas import tpu as pltpu
from jax.sharding import PartitionSpec as P

HD = 128
GRP = 2
BLK = 256
NEG = -1e30
MESH = pl.DeviceIdType.MESH
F32 = jnp.float32
BF16 = jnp.bfloat16
LOG2E = math.log2(math.e)


def owner_seq(p, rl):
    return 4 * rl + lax.rem(p + rl + 1, 4)


def owner_of_static(s):
    rl = s // 4
    p = (s % 4 - rl - 1) % 4
    return p, rl


def await_bytes(ref, sem):
    pltpu.make_async_copy(ref, ref, sem).wait()


def dot_t(a, b):
    return lax.dot_general(a, b, (((1,), (1,)), ((), ())), preferred_element_type=F32)


def kernel(
    ns, nh, table, teacher, student, loss, grads,
    got0, got1, got2, flat0, flat1, flat2, stage0, stage1, stage2,
    t_all, s_all, s_turn, log_s, prob_s, work, col, back, l_mine, l_seq, l_head,
    p1_send, p1_recv, s_send, s_recv, p2_send, t_recv, g_send, g_recv, l_send, l_recv,
):
    rows = teacher.shape[1]
    width = teacher.shape[2]
    slots = width // HD
    sub = rows // nh
    rels = student.shape[2] // HD
    rel_all = rels * nh
    tokens = rows * ns
    blocks = tokens // BLK
    per_blk = BLK // rows
    me_s = lax.axis_index("seq")
    me_g = lax.axis_index("head")
    my_rl = me_s // 4
    my_p = lax.rem(lax.rem(me_s, 4) - my_rl + 7, 4)
    active = my_p < 3
    got = (got0, got1, got2)
    flat = (flat0, flat1, flat2)
    stage = (stage0, stage1, stage2)

    def send(src, dst, ssem, rsem, s, g):
        pltpu.make_async_remote_copy(
            src_ref=src, dst_ref=dst, send_sem=ssem, recv_sem=rsem,
            device_id=(s, g), device_id_type=MESH,
        ).start()

    for p in range(3):
        for step in range(1, nh):
            g = lax.rem(me_g + step, nh)
            send(
                teacher.at[p, pl.ds(g * sub, sub), :], got[p].at[me_g],
                p1_send, p1_recv.at[p], me_s, g,
            )
        pltpu.make_async_copy(
            teacher.at[p, pl.ds(me_g * sub, sub), :], got[p].at[me_g], p1_recv.at[p]
        ).start()

    def student_out(i, c):
        q = lax.rem(i + me_s, 3 * rels)
        p = q // rels
        rl = lax.rem(q, rels)
        s = owner_seq(p, rl)
        src = student.at[p, :, pl.ds(pl.multiple_of(rl * HD, HD), HD)]
        dst = s_all.at[pl.ds(pl.multiple_of(me_s * rows, rows), rows), :]

        @pl.when(s != me_s)
        def _():
            send(src, dst, s_send, s_recv, s, me_g)

        @pl.when(s == me_s)
        def _():
            pltpu.make_async_copy(src, dst, s_recv).start()

        return c

    lax.fori_loop(0, 3 * rels, student_out, 0)

    for p in range(3):
        await_bytes(got[p], p1_recv.at[p])
        for h in range(slots * nh):
            lane = h % slots * HD
            flat[p][h] = got[p][h // slots, :, lane : lane + HD]

        def relation_out(i, c):
            r = lax.rem(i + 2 * me_s + rels * me_g, rel_all)
            for k in range(GRP):
                stage[p][r, :, k * HD : (k + 1) * HD] = flat[p][table[GRP * r + k]]
            g = r // rels
            s = owner_seq(p, lax.rem(r, rels))
            src = stage[p].at[r]
            dst = t_all.at[pl.ds(pl.multiple_of(me_s * rows + me_g * sub, sub), sub), :]
            here = jnp.logical_and(s == me_s, g == me_g)

            @pl.when(jnp.logical_not(here))
            def _():
                send(src, dst, p2_send, t_recv, s, g)

            @pl.when(here)
            def _():
                pltpu.make_async_copy(src, dst, t_recv).start()

            return c

        lax.fori_loop(0, rel_all, relation_out, 0)

    scale_t = LOG2E / math.sqrt(GRP * HD)
    scale_s = LOG2E / math.sqrt(HD)
    key_row = lax.broadcasted_iota(jnp.int32, (BLK, BLK), 0)
    query_col = lax.broadcasted_iota(jnp.int32, (BLK, BLK), 1)

    def at_block(b):
        return pl.ds(pl.multiple_of(b * BLK, BLK), BLK)

    def fold(op, x):
        return op(x.reshape(BLK // 8, 8, BLK), axis=0)

    @pl.when(active)
    def _():
        await_bytes(s_all, s_recv)

        def turn(b, c):
            s_turn[:, at_block(b)] = s_all[at_block(b), :].T
            col[at_block(b), :] = jnp.zeros((BLK, HD), F32)
            return c

        lax.fori_loop(0, blocks, turn, 0)

        def student_block(qb, c):
            base = qb * (qb + 1) // 2
            query = s_all[at_block(qb), :]

            def first(kb, top):
                logit = dot_t(s_all[at_block(kb), :], query) * scale_s
                log_s[base + kb] = logit
                return jnp.maximum(top, fold(jnp.max, logit))

            top = lax.fori_loop(0, qb, first, jnp.full((8, BLK), NEG, F32))
            logit = jnp.where(key_row <= query_col, dot_t(query, query) * scale_s, NEG)
            log_s[base + qb] = logit
            top = jnp.max(jnp.maximum(top, fold(jnp.max, logit)), axis=0, keepdims=True)

            def second(kb, total):
                weight = jnp.exp2(log_s[base + kb] - top)
                prob_s[base + kb] = weight
                return total + fold(jnp.sum, weight)

            total = lax.fori_loop(0, qb + 1, second, jnp.zeros((8, BLK), F32))
            total = jnp.sum(total, axis=0, keepdims=True)
            inverse = 1.0 / total
            lse = top + jnp.log2(total)

            def third(kb, c):
                log_s[base + kb] = log_s[base + kb] - lse
                prob_s[base + kb] = prob_s[base + kb] * inverse
                return c

            lax.fori_loop(0, qb + 1, third, 0)
            return c

        lax.fori_loop(0, blocks, student_block, 0)

        await_bytes(t_all, t_recv)

        def teacher_block(i, loss_row):
            qb = blocks - 1 - i
            base = qb * (qb + 1) // 2
            query = t_all[at_block(qb), :]

            def first(kb, top):
                logit = dot_t(t_all[at_block(kb), :], query) * scale_t
                work[kb] = logit
                return jnp.maximum(top, fold(jnp.max, logit))

            top = lax.fori_loop(0, qb, first, jnp.full((8, BLK), NEG, F32))
            logit = jnp.where(key_row <= query_col, dot_t(query, query) * scale_t, NEG)
            work[qb] = logit
            top = jnp.max(jnp.maximum(top, fold(jnp.max, logit)), axis=0, keepdims=True)

            def second(kb, carried):
                total, cross = carried
                shifted = work[kb] - top
                weight = jnp.exp2(shifted)
                work[kb] = weight
                return (
                    total + fold(jnp.sum, weight),
                    cross + fold(jnp.sum, weight * (shifted - log_s[base + kb])),
                )

            zero = jnp.zeros((8, BLK), F32)
            total, cross = lax.fori_loop(0, qb + 1, second, (zero, zero))
            total = jnp.sum(total, axis=0, keepdims=True)
            cross = jnp.sum(cross, axis=0, keepdims=True)
            inverse = 1.0 / total
            query_s = s_all[at_block(qb), :]

            def third(kb, row):
                diff = (prob_s[base + kb] - work[kb] * inverse).astype(BF16)
                col[at_block(kb), :] += jnp.dot(diff, query_s, preferred_element_type=F32)
                return row + jnp.dot(s_turn[:, at_block(kb)], diff, preferred_element_type=F32)

            row = lax.fori_loop(0, qb + 1, third, jnp.zeros((HD, BLK), F32))
            block = (col[at_block(qb), :] + row.T) * (1.0 / math.sqrt(HD))
            back[at_block(qb), :] = block.astype(BF16)
            for j in range(per_blk):
                s = qb * per_blk + j
                src = back.at[pl.ds(pl.multiple_of(s * rows, rows), rows), :]
                dst = grads.at[my_p, :, pl.ds(pl.multiple_of(my_rl * HD, HD), HD)]

                @pl.when(s != me_s)
                def _():
                    send(src, dst, g_send, g_recv, s, me_g)

                @pl.when(s == me_s)
                def _():
                    pltpu.make_async_copy(src, dst, g_recv).start()

            return loss_row + (cross * inverse - jnp.log2(total))

        loss_row = lax.fori_loop(0, blocks, teacher_block, jnp.zeros((1, BLK), F32))
        mine = jnp.full((8, HD), jnp.sum(loss_row), F32)
        l_mine[...] = mine
        l_seq[me_s] = mine

        def loss_out(i, c):
            s = lax.rem(me_s + 1 + i, ns)
            send(l_mine, l_seq.at[me_s], l_send.at[0], l_recv.at[0], s, me_g)
            return c

        lax.fori_loop(0, ns - 1, loss_out, 0)
        await_bytes(l_seq.at[pl.ds(0, 3 * rels - 1)], l_recv.at[0])

    @pl.when(jnp.logical_not(active))
    def _():
        await_bytes(l_seq.at[pl.ds(0, 3 * rels)], l_recv.at[0])

    group = jnp.zeros((8, HD), F32)
    for s in range(ns):
        if owner_of_static(s)[0] < 3:
            group = group + l_seq[s]
    l_head[me_g] = group
    for step in range(1, nh):
        send(l_head.at[me_g], l_head.at[me_g], l_send.at[1], l_recv.at[1], me_s, lax.rem(me_g + step, nh))
    await_bytes(l_head.at[pl.ds(0, nh - 1)], l_recv.at[1])
    total = l_head[0]
    for g in range(1, nh):
        total = total + l_head[g]
    loss[0] = total[0, 0] * (1.0 / (LOG2E * 3.0 * rel_all * tokens))

    await_bytes(grads, g_recv)
    await_bytes(teacher.at[:, pl.ds(0, rows - sub), :], p1_send)

    @pl.when(active)
    def _():
        await_bytes(back.at[pl.ds(0, (3 * rels - 1) * rows), :], s_send)
        await_bytes(back.at[pl.ds(0, (ns - 1) * rows), :], g_send)
        await_bytes(t_all.at[pl.ds(0, (3 * rel_all - 1) * sub), :], p2_send)
        await_bytes(l_seq.at[pl.ds(0, ns - 1)], l_send.at[0])

    @pl.when(jnp.logical_not(active))
    def _():
        await_bytes(back.at[pl.ds(0, 3 * rels * rows), :], s_send)
        await_bytes(t_all.at[pl.ds(0, 3 * rel_all * sub), :], p2_send)

    await_bytes(l_head.at[pl.ds(0, nh - 1)], l_send.at[1])


def solution(mesh):
    ns = mesh.shape["seq"]
    nh = mesh.shape["head"]

    def body(teacher, student, table):
        rows, _, width = teacher.shape
        swidth = student.shape[2]
        sub = rows // nh
        rel_all = swidth // HD * nh
        tokens = rows * ns
        blocks = tokens // BLK
        tiles = blocks * (blocks + 1) // 2
        dma = pltpu.SemaphoreType.DMA
        loss, grads = pl.pallas_call(
            functools.partial(kernel, ns, nh),
            out_shape=(
                jax.ShapeDtypeStruct((1,), F32),
                jax.ShapeDtypeStruct((3, rows, swidth), BF16),
            ),
            in_specs=[
                pl.BlockSpec(memory_space=pltpu.SMEM),
                pl.BlockSpec(memory_space=pl.ANY),
                pl.BlockSpec(memory_space=pl.ANY),
            ],
            out_specs=(
                pl.BlockSpec(memory_space=pltpu.SMEM),
                pl.BlockSpec(memory_space=pl.ANY),
            ),
            scratch_shapes=[pltpu.VMEM((nh, sub, width), BF16)] * 3
            + [pltpu.VMEM((width // HD * nh, sub, HD), BF16)] * 3
            + [pltpu.VMEM((rel_all, sub, GRP * HD), BF16)] * 3
            + [
                pltpu.VMEM((tokens, GRP * HD), BF16),
                pltpu.VMEM((tokens, HD), BF16),
                pltpu.VMEM((HD, tokens), BF16),
                pltpu.VMEM((tiles, BLK, BLK), F32),
                pltpu.VMEM((tiles, BLK, BLK), F32),
                pltpu.VMEM((blocks, BLK, BLK), F32),
                pltpu.VMEM((tokens, HD), F32),
                pltpu.VMEM((tokens, HD), BF16),
                pltpu.VMEM((8, HD), F32),
                pltpu.VMEM((ns, 8, HD), F32),
                pltpu.VMEM((nh, 8, HD), F32),
                dma, dma((3,)), dma, dma, dma, dma, dma, dma, dma((2,)), dma((2,)),
            ],
            compiler_params=pltpu.CompilerParams(
                has_side_effects=True, vmem_limit_bytes=48 * 1024 * 1024
            ),
            cost_estimate=pl.CostEstimate(
                flops=tokens * tokens * 1280, bytes_accessed=4 * 1024 * 1024,
                transcendentals=tokens * tokens,
            ),
            name="relations",
        )(table, jnp.transpose(teacher, (1, 0, 2)), jnp.transpose(student, (1, 0, 2)))
        return loss.reshape(()), jnp.transpose(grads, (1, 0, 2))

    return jax.shard_map(
        body,
        mesh=mesh,
        in_specs=(P("seq", None, "head"), P("seq", None, "head"), P()),
        out_specs=(P(), P("seq", None, "head")),
        check_vma=False,
    )
```

time: 474 us -> 79.5 us (0.17)
  waiting for transfers between devices: 209 us -> 0 us
  blocking collectives: 83.6 us -> 0 us
  matrix products: 79 us -> 0 us
  Pallas kernels: 0 us -> 73.3 us
  local copies, waits for them, and re-layouts: 73.5 us -> 3.52 us
  between operations: 15.7 us -> 2.38 us
  other arithmetic: 11 us -> 0 us
    all_gather x3 -> x0, waiting for transfers between devices: 209 us -> none  [the longest x1 90.3 us: body(): shard_part = lax.all_gather(teacher, 'head', axis=2, tiled=True)]
    dot_general x25 -> x0, matrix products: 79 us -> none  [the longest x4 24.2 us: backward_step(): jnp.einsum('ahqk,kahd->qahd', diff, key_stud, preferred_element_type=jnp....]
    pallas_call x0 -> x1, Pallas kernels: none -> 73.3 us  [body(): pl.pallas_call(functools.partial(kernel, ns, nh), out_shape=(jax.ShapeDty...]
    psum x1 -> x0, blocking collectives: 64.8 us -> none  [body(): kl_total = lax.psum(jnp.sum(kl_rows), ('seq', 'head'))]
    dynamic_slice x25 -> x0, local copies, waits for them, and re-layouts: 56.7 us -> none  [the longest x8 23.4 us: logits(): lax.dynamic_slice_in_dim(all_teach, first_key, span_rows, 0)]
    all_gather x1 -> x0, blocking collectives: 18.8 us -> none  [body(): lax.all_gather(jnp.stack([lse_teach, lse_stud], 0), 'seq', axis=3, tiled=...]
    reshape x1 -> x0, local copies, waits for them, and re-layouts: 9.11 us -> none  [body(): blocks = shard_part.reshape(rows_here, 3, held, HD)]
    reduce_sum x5 -> x0, other arithmetic: 7.74 us -> none  [the longest x4 7.13 us: forward_step(): jnp.sum(weights * jnp.where(allowed, teach_logit - stud_logit, 0.0), axis...]
  transfers between devices with their start and end apart: 3 -> 0, of which waited for: 3 -> 0; matrix products, arithmetic and copies ran while one was open for 4% -> 0% of each run, Pallas kernels for 0% -> 0%
where the time goes in v1:
time: 79.5 us; the launch traced here: 79.3 us
  Pallas kernels  73.3 us (92%)
  local copies, waits for them, and re-layouts  3.52 us (4%)
  between operations  2.38 us (3%)
    pallas_call x1, Pallas kernels, body(): pl.pallas_call(functools.partial(kernel, ns, nh), out_shape=(jax.ShapeDty...  73.3 us
    unnamed x7, local copies, waits for them, and re-layouts  3.52 us

profile of v1, /device:TPU:1, one launch (start us, length us, event | category | flops | bytes accessed | tf_op | source)
XLA Modules:
  0.0 79.3 jit_solution(17787443732535418368)
XLA Ops:
  0.6 0.0 copy-start.2
  0.6 0.6 copy-done.2
  1.3 0.0 copy-start
  1.3 1.1 %copy-done = bf16[128,3,1024]{2,0,1:T(8,128)(2,1)S(1)} copy-done((bf16[128,3,1024]{2,0,1:T(8,128)(2,1)S(1)}, bf16[128,3,1024]{2,0,1:T(8,128)(2,1)}, u32[]{:S(2)}) %copy-start) | copy-done | bytes 786456
  2.4 0.0 copy-start.1
  2.4 1.0 %copy-done.1 = bf16[128,3,512]{2,0,1:T(8,128)(2,1)S(1)} copy-done((bf16[128,3,512]{2,0,1:T(8,128)(2,1)S(1)}, bf16[128,3,512]{2,0,1:T(8,128)(2,1)}, u32[]{:S(2)}) %copy-start.1) | copy-done | bytes 393240
  3.4 73.3 %relations.1 = (f32[1]{0:T(128)}, bf16[3,128,512]{2,1,0:T(8,128)(2,1)S(1)}) custom-call(s32[64]{0:T(128)S(1)} %copy-done.2, bf16[3,128,1024]{2,1,0:T(8,128)(2,1)S(1)} %bitcast.5, bf16[3,128,512]{2,1,0:T(8,128)(2,1)S(1)} %bitcast.6), custom_call_target="tpu_custom_call" | custom-call | flops 5368709120 | bytes 4194304 | tf_op jit(solution)/shard_map/relations/pallas_call | solution.py:302
  77.4 0.7 copy.8
Async XLA Ops:
  0.6 0.7 copy-start.2
  1.3 1.1 %copy-start = (bf16[128,3,1024]{2,0,1:T(8,128)(2,1)S(1)}, bf16[128,3,1024]{2,0,1:T(8,128)(2,1)}, u32[]{:S(2)}) copy-start(bf16[128,3,1024]{2,0,1:T(8,128)(2,1)} %param.3) | copy-start | bytes 2359300
  2.4 1.0 %copy-start.1 = (bf16[128,3,512]{2,0,1:T(8,128)(2,1)S(1)}, bf16[128,3,512]{2,0,1:T(8,128)(2,1)}, u32[]{:S(2)}) copy-start(bf16[128,3,512]{2,0,1:T(8,128)(2,1)} %param.4) | copy-start | bytes 1179652

commit v2 on v1

v2 whole, which is shorter than its diff:
```python
import functools
import math

import jax
import jax.numpy as jnp
from jax import lax
from jax.experimental import pallas as pl
from jax.experimental.pallas import tpu as pltpu
from jax.sharding import PartitionSpec as P

HD = 128
GRP = 2
BLK = 256
NEG = -1e30
MESH = pl.DeviceIdType.MESH
F32 = jnp.float32
BF16 = jnp.bfloat16
LOG2E = math.log2(math.e)


def owner_seq(p, rl):
    return 4 * rl + lax.rem(p + rl + 1, 4)


def owner_of_static(s):
    rl = s // 4
    p = (s % 4 - rl - 1) % 4
    return p, rl


def await_bytes(ref, sem):
    pltpu.make_async_copy(ref, ref, sem).wait()


def dot_t(a, b):
    return lax.dot_general(a, b, (((1,), (1,)), ((), ())), preferred_element_type=F32)


def kernel(
    ns, nh, table_hbm, teacher, student, loss, grads, table,
    got0, got1, got2, flat0, flat1, flat2, stage0, stage1, stage2,
    t_all, s_all, s_turn, log_s, w_s, w_t, top_s, top_t, lse_s, lse_t, col, back,
    l_mine, l_seq, l_head,
    tab_sem, p1_send, p1_recv, s_send, s_recv, p2_send, t_recv, g_send, g_recv, l_send, l_recv, all_in,
):
    rows = teacher.shape[1]
    width = teacher.shape[2]
    slots = width // HD
    sub = rows // nh
    rels = student.shape[2] // HD
    rel_all = rels * nh
    tokens = rows * ns
    wide = tokens // (2 * BLK)
    per_blk = 2 * BLK // rows
    me_s = lax.axis_index("seq")
    me_g = lax.axis_index("head")
    my_rl = me_s // 4
    my_p = lax.rem(lax.rem(me_s, 4) - my_rl + 7, 4)
    active = my_p < 3
    got = (got0, got1, got2)
    flat = (flat0, flat1, flat2)
    stage = (stage0, stage1, stage2)

    def send(src, dst, ssem, rsem, s, g):
        pltpu.make_async_remote_copy(
            src_ref=src, dst_ref=dst, send_sem=ssem, recv_sem=rsem,
            device_id=(s, g), device_id_type=MESH,
        ).start()

    barrier = pltpu.get_barrier_semaphore()

    def greet(sem, along_seq):
        def one(i, c):
            if along_seq:
                to = (lax.rem(me_s + i, ns), me_g)
            else:
                to = (me_s, lax.rem(me_g + i, nh))
            pl.semaphore_signal(sem, inc=1, device_id=to, device_id_type=MESH)
            return c

        lax.fori_loop(1, ns if along_seq else nh, one, 0)

    greet(barrier, False)
    greet(barrier, True)
    table_copy = pltpu.make_async_copy(table_hbm, table, tab_sem)
    table_copy.start()
    pl.semaphore_wait(barrier, ns + nh - 2)

    for p in range(3):
        for step in range(1, nh):
            g = lax.rem(me_g + step, nh)
            send(
                teacher.at[p, pl.ds(g * sub, sub), :], got[p].at[me_g],
                p1_send, p1_recv.at[p], me_s, g,
            )
        pltpu.make_async_copy(
            teacher.at[p, pl.ds(me_g * sub, sub), :], got[p].at[me_g], p1_recv.at[p]
        ).start()

    greet(all_in, False)

    def student_out(i, c):
        q = lax.rem(i + me_s, 3 * rels)
        p = q // rels
        rl = lax.rem(q, rels)
        s = owner_seq(p, rl)
        src = student.at[p, :, pl.ds(pl.multiple_of(rl * HD, HD), HD)]
        dst = s_all.at[pl.ds(pl.multiple_of(me_s * rows, rows), rows), :]

        @pl.when(s != me_s)
        def _():
            send(src, dst, s_send, s_recv, s, me_g)

        @pl.when(s == me_s)
        def _():
            pltpu.make_async_copy(src, dst, s_recv).start()

        return c

    lax.fori_loop(0, 3 * rels, student_out, 0)
    table_copy.wait()
    pl.semaphore_wait(all_in, nh - 1)

    for p in range(3):
        await_bytes(got[p], p1_recv.at[p])
        for h in range(slots * nh):
            lane = h % slots * HD
            flat[p][h] = got[p][h // slots, :, lane : lane + HD]

        def relation_out(i, c):
            r = lax.rem(i + 2 * me_s + rels * me_g, rel_all)
            for k in range(GRP):
                stage[p][r, :, k * HD : (k + 1) * HD] = flat[p][table[GRP * r + k]]
            g = r // rels
            s = owner_seq(p, lax.rem(r, rels))
            src = stage[p].at[r]
            dst = t_all.at[pl.ds(pl.multiple_of(me_s * rows + me_g * sub, sub), sub), :]
            here = jnp.logical_and(s == me_s, g == me_g)

            @pl.when(jnp.logical_not(here))
            def _():
                send(src, dst, p2_send, t_recv, s, g)

            @pl.when(here)
            def _():
                pltpu.make_async_copy(src, dst, t_recv).start()

            return c

        lax.fori_loop(0, rel_all, relation_out, 0)

    scale_t = LOG2E / math.sqrt(GRP * HD)
    scale_s = LOG2E / math.sqrt(HD)
    key_row = lax.broadcasted_iota(jnp.int32, (BLK, BLK), 0)
    query_col = lax.broadcasted_iota(jnp.int32, (BLK, BLK), 1)
    deep = (BLK // 8, 8, BLK)

    def at_block(b):
        return pl.ds(pl.multiple_of(b * BLK, BLK), BLK)

    def tile_of(kb, qb):
        return qb * (qb + 1) // 2 + kb

    def logits(feats, kb, query, scale, diagonal):
        out = dot_t(feats[at_block(kb), :], query) * scale
        if diagonal:
            out = jnp.where(key_row <= query_col, out, NEG)
        return out.reshape(deep)

    def student_tile(kb, qb, query, state, diagonal):
        top, total = state
        t = tile_of(kb, qb)
        logit = logits(s_all, kb, query, scale_s, diagonal)
        new = jnp.maximum(top, jnp.max(logit, axis=0))
        weight = jnp.exp2(logit - new)
        log_s[t] = logit.reshape(BLK, BLK)
        w_s[t] = weight.reshape(BLK, BLK)
        top_s[t] = new
        return new, total * jnp.exp2(top - new) + jnp.sum(weight, axis=0)

    def teacher_tile(kb, qb, query, state, diagonal):
        top, total, cross = state
        t = tile_of(kb, qb)
        logit = logits(t_all, kb, query, scale_t, diagonal)
        new = jnp.maximum(top, jnp.max(logit, axis=0))
        weight = jnp.exp2(logit - new)
        w_t[t] = weight.reshape(BLK, BLK)
        top_t[t] = new
        again = jnp.exp2(top - new)
        gap = logit - log_s[t].reshape(deep)
        return (
            new,
            total * again + jnp.sum(weight, axis=0),
            cross * again + jnp.sum(weight * gap, axis=0),
        )

    def sweep(tile, feats, wq, fresh):
        qa, qb = 2 * wq, 2 * wq + 1
        query_a, query_b = feats[at_block(qa), :], feats[at_block(qb), :]

        def full(i, c):
            state_a, state_b = c
            for kb in (2 * i, 2 * i + 1):
                state_a = tile(kb, qa, query_a, state_a, False)
                state_b = tile(kb, qb, query_b, state_b, False)
            return state_a, state_b

        state_a, state_b = fresh, fresh
        for i in range(wq):
            state_a, state_b = full(i, (state_a, state_b))
        state_a = tile(qa, qa, query_a, state_a, True)
        state_b = tile(qa, qb, query_b, state_b, False)
        state_b = tile(qb, qb, query_b, state_b, True)
        return (qa, state_a), (qb, state_b)

    def loop(n, f, init):
        for i in range(n):
            init = f(i, init)
        return init

    low = jnp.full((8, BLK), NEG, F32)
    zero = jnp.zeros((8, BLK), F32)

    @pl.when(active)
    def _():
        await_bytes(s_all, s_recv)

        def turn(b, c):
            s_turn[:, at_block(b)] = s_all[at_block(b), :].T
            col[at_block(b), :] = jnp.zeros((BLK, HD), F32)
            return c

        lax.fori_loop(0, 2 * wide, turn, 0)

        def student_block(wq, c):
            for q, (top, total) in sweep(student_tile, s_all, wq, (low, zero)):
                peak = jnp.max(top, axis=0, keepdims=True)
                total = jnp.sum(total * jnp.exp2(top - peak), axis=0, keepdims=True)
                lse_s[q] = jnp.broadcast_to(peak + jnp.log2(total), (8, BLK))
            return c

        loop(wide, student_block, 0)

        await_bytes(t_all, t_recv)

        def teacher_block(wq, loss_row):
            for q, (top, total, cross) in sweep(teacher_tile, t_all, wq, (low, zero, zero)):
                peak = jnp.max(top, axis=0, keepdims=True)
                again = jnp.exp2(top - peak)
                total = jnp.sum(total * again, axis=0, keepdims=True)
                cross = jnp.sum(cross * again, axis=0, keepdims=True)
                lse = jnp.broadcast_to(peak + jnp.log2(total), (8, BLK))
                lse_t[q] = lse
                loss_row = loss_row + (cross / total - lse + lse_s[q])
            return loss_row

        loss_row = loop(wide, teacher_block, zero)
        mine = jnp.full((8, HD), jnp.sum(loss_row) * 0.125, F32)
        l_mine[...] = mine
        l_seq[me_s] = mine

        def loss_out(i, c):
            s = lax.rem(me_s + 1 + i, ns)
            send(l_mine, l_seq.at[me_s], l_send.at[0], l_recv.at[0], s, me_g)
            return c

        lax.fori_loop(0, ns - 1, loss_out, 0)

        def diff(kb, q):
            t = tile_of(kb, q)
            ours = w_s[t].reshape(deep) * jnp.exp2(top_s[t] - lse_s[q])
            theirs = w_t[t].reshape(deep) * jnp.exp2(top_t[t] - lse_t[q])
            return (ours - theirs).reshape(BLK, BLK).astype(BF16)

        def add(kb, q, query, row):
            d = diff(kb, q)
            col[at_block(kb), :] += jnp.dot(d, query, preferred_element_type=F32)
            return row + jnp.dot(s_turn[:, at_block(kb)], d, preferred_element_type=F32)

        def grad_block(step, c):
            wq = wide - 1 - step
            qa, qb = 2 * wq, 2 * wq + 1
            query_a, query_b = s_all[at_block(qa), :], s_all[at_block(qb), :]

            def full(i, c):
                row_a, row_b = c
                for kb in (2 * i, 2 * i + 1):
                    row_a = add(kb, qa, query_a, row_a)
                    row_b = add(kb, qb, query_b, row_b)
                return row_a, row_b

            none = jnp.zeros((HD, BLK), F32)
            row_a, row_b = none, none
            for i in range(wq):
                row_a, row_b = full(i, (row_a, row_b))
            row_a = add(qa, qa, query_a, row_a)
            row_b = add(qa, qb, query_b, row_b)
            row_b = add(qb, qb, query_b, row_b)
            for q, row in ((qa, row_a), (qb, row_b)):
                block = (col[at_block(q), :] + row.T) * (1.0 / math.sqrt(HD))
                back[at_block(q), :] = block.astype(BF16)
            for j in range(per_blk):
                s = wq * per_blk + j
                src = back.at[pl.ds(pl.multiple_of(s * rows, rows), rows), :]
                dst = grads.at[my_p, :, pl.ds(pl.multiple_of(my_rl * HD, HD), HD)]

                @pl.when(s != me_s)
                def _():
                    send(src, dst, g_send, g_recv, s, me_g)

                @pl.when(s == me_s)
                def _():
                    pltpu.make_async_copy(src, dst, g_recv).start()

            return c

        loop(wide, grad_block, 0)
        await_bytes(l_seq.at[pl.ds(0, 3 * rels - 1)], l_recv.at[0])

    @pl.when(jnp.logical_not(active))
    def _():
        await_bytes(l_seq.at[pl.ds(0, 3 * rels)], l_recv.at[0])

    group = jnp.zeros((8, HD), F32)
    for s in range(ns):
        if owner_of_static(s)[0] < 3:
            group = group + l_seq[s]
    l_head[me_g] = group
    for step in range(1, nh):
        send(l_head.at[me_g], l_head.at[me_g], l_send.at[1], l_recv.at[1], me_s, lax.rem(me_g + step, nh))
    await_bytes(grads, g_recv)
    await_bytes(l_head.at[pl.ds(0, nh - 1)], l_recv.at[1])
    total = l_head[0]
    for g in range(1, nh):
        total = total + l_head[g]
    loss[0] = total[0, 0] * (1.0 / (LOG2E * 3.0 * rel_all * tokens))

    await_bytes(teacher.at[:, pl.ds(0, rows - sub), :], p1_send)

    @pl.when(active)
    def _():
        await_bytes(back.at[pl.ds(0, (3 * rels - 1) * rows), :], s_send)
        await_bytes(back.at[pl.ds(0, (ns - 1) * rows), :], g_send)
        await_bytes(t_all.at[pl.ds(0, (3 * rel_all - 1) * sub), :], p2_send)
        await_bytes(l_seq.at[pl.ds(0, ns - 1)], l_send.at[0])

    @pl.when(jnp.logical_not(active))
    def _():
        await_bytes(back.at[pl.ds(0, 3 * rels * rows), :], s_send)
        await_bytes(t_all.at[pl.ds(0, 3 * rel_all * sub), :], p2_send)

    await_bytes(l_head.at[pl.ds(0, nh - 1)], l_send.at[1])


def solution(mesh):
    ns = mesh.shape["seq"]
    nh = mesh.shape["head"]

    def body(teacher, student, table):
        rows, _, width = teacher.shape
        swidth = student.shape[2]
        sub = rows // nh
        rel_all = swidth // HD * nh
        tokens = rows * ns
        blocks = tokens // BLK
        tiles = blocks * (blocks + 1) // 2
        dma = pltpu.SemaphoreType.DMA
        loss, grads = pl.pallas_call(
            functools.partial(kernel, ns, nh),
            out_shape=(
                jax.ShapeDtypeStruct((1,), F32),
                jax.ShapeDtypeStruct((3, rows, swidth), BF16),
            ),
            in_specs=[
                pl.BlockSpec(memory_space=pltpu.HBM),
                pl.BlockSpec(memory_space=pltpu.HBM),
                pl.BlockSpec(memory_space=pltpu.HBM),
            ],
            out_specs=(
                pl.BlockSpec(memory_space=pltpu.SMEM),
                pl.BlockSpec(memory_space=pltpu.HBM),
            ),
            scratch_shapes=[pltpu.SMEM(table.shape, jnp.int32)]
            + [pltpu.VMEM((nh, sub, width), BF16)] * 3
            + [pltpu.VMEM((width // HD * nh, sub, HD), BF16)] * 3
            + [pltpu.VMEM((rel_all, sub, GRP * HD), BF16)] * 3
            + [
                pltpu.VMEM((tokens, GRP * HD), BF16),
                pltpu.VMEM((tokens, HD), BF16),
                pltpu.VMEM((HD, tokens), BF16),
                pltpu.VMEM((tiles, BLK, BLK), F32),
                pltpu.VMEM((tiles, BLK, BLK), F32),
                pltpu.VMEM((tiles, BLK, BLK), F32),
                pltpu.VMEM((tiles, 8, BLK), F32),
                pltpu.VMEM((tiles, 8, BLK), F32),
                pltpu.VMEM((blocks, 8, BLK), F32),
                pltpu.VMEM((blocks, 8, BLK), F32),
                pltpu.VMEM((tokens, HD), F32),
                pltpu.VMEM((tokens, HD), BF16),
                pltpu.VMEM((8, HD), F32),
                pltpu.VMEM((ns, 8, HD), F32),
                pltpu.VMEM((nh, 8, HD), F32),
                dma, dma, dma((3,)), dma, dma, dma, dma, dma, dma, dma((2,)), dma((2,)),
                pltpu.SemaphoreType.REGULAR,
            ],
            compiler_params=pltpu.CompilerParams(
                has_side_effects=True, collective_id=0, vmem_limit_bytes=60 * 1024 * 1024
            ),
            cost_estimate=pl.CostEstimate(
                flops=tokens * tokens * 1280, bytes_accessed=4 * 1024 * 1024,
                transcendentals=tokens * tokens,
            ),
            name="relations",
        )(table, jnp.transpose(teacher, (1, 0, 2)), jnp.transpose(student, (1, 0, 2)))
        return loss.reshape(()), jnp.transpose(grads, (1, 0, 2))

    return jax.shard_map(
        body,
        mesh=mesh,
        in_specs=(P("seq", None, "head"), P("seq", None, "head"), P()),
        out_specs=(P(), P("seq", None, "head")),
        check_vma=False,
    )
```

time: 79.5 us -> 53.1 us (0.67)
  Pallas kernels: 73.3 us -> 48.5 us
  local copies, waits for them, and re-layouts: 3.52 us -> 1.77 us
    pallas_call x1, Pallas kernels: 73.3 us -> 48.5 us  [body(): pl.pallas_call(functools.partial(kernel, ns, nh), out_shape=(jax.ShapeDty...]
    unnamed x7 -> x1, local copies, waits for them, and re-layouts: 3.52 us -> 1.77 us
where the time goes in v2:
time: 53.1 us; the launch traced here: 52.6 us
  Pallas kernels  48.5 us (91%)
  between operations  2.39 us (5%)
  local copies, waits for them, and re-layouts  1.77 us (3%)
    pallas_call x1, Pallas kernels, body(): pl.pallas_call(functools.partial(kernel, ns, nh), out_shape=(jax.ShapeDty...  48.5 us
    unnamed x1, local copies, waits for them, and re-layouts  1.77 us

profile of v2, /device:TPU:1, one launch (start us, length us, event | category | flops | bytes accessed | tf_op | source)
XLA Modules:
  0.0 52.6 jit_solution(12000894652897252269)
XLA Ops:
  0.6 48.5 %relations.1 = (f32[1]{0:T(128)}, bf16[3,128,512]{2,1,0:T(8,128)(2,1)}) custom-call(s32[64]{0:T(128)} %table_hbm.1, bf16[3,128,1024]{2,1,0:T(8,128)(2,1)} %bitcast.5, bf16[3,128,512]{2,1,0:T(8,128)(2,1)} %bitcast.6), custom_call_target="tpu_custom_call" | custom-call | flops 5368709120 | bytes 4194304 | tf_op jit(solution)/shard_map/relations/pallas_call | solution.py:368
  49.7 1.8 %copy.8 = bf16[128,3,512]{2,0,1:T(8,128)(2,1)} copy(bf16[128,3,512]{2,0,1:T(8,128)(2,1)} %bitcast.4) | data formatting | bytes 786432

commit v3 on v2

--- a/solution.py
+++ b/solution.py
@@ -11,6 +11,7 @@
 HD = 128
 GRP = 2
 BLK = 256
+CH = 256
 NEG = -1e30
 MESH = pl.DeviceIdType.MESH
 F32 = jnp.float32
@@ -39,7 +40,7 @@
 def kernel(
     ns, nh, table_hbm, teacher, student, loss, grads, table,
     got0, got1, got2, flat0, flat1, flat2, stage0, stage1, stage2,
-    t_all, s_all, s_turn, log_s, w_s, w_t, top_s, top_t, lse_s, lse_t, col, back,
+    t_all, s_all, s_turn, log_s, w_s, w_t, top_s, top_t, lse_s, lse_t, rows_turned, back,
     l_mine, l_seq, l_head,
     tab_sem, p1_send, p1_recv, s_send, s_recv, p2_send, t_recv, g_send, g_recv, l_send, l_recv, all_in,
 ):
@@ -139,11 +140,11 @@
 
             @pl.when(jnp.logical_not(here))
             def _():
-                send(src, dst, p2_send, t_recv, s, g)
+                send(src, dst, p2_send, t_recv.at[me_s // per_blk], s, g)
 
             @pl.when(here)
             def _():
-                pltpu.make_async_copy(src, dst, t_recv).start()
+                pltpu.make_async_copy(src, dst, t_recv.at[me_s // per_blk]).start()
 
             return c
 
@@ -153,7 +154,7 @@
     scale_s = LOG2E / math.sqrt(HD)
     key_row = lax.broadcasted_iota(jnp.int32, (BLK, BLK), 0)
     query_col = lax.broadcasted_iota(jnp.int32, (BLK, BLK), 1)
-    deep = (BLK // 8, 8, BLK)
+    deep = (CH // 8, 8, BLK)
 
     def at_block(b):
         return pl.ds(pl.multiple_of(b * BLK, BLK), BLK)
@@ -165,34 +166,35 @@
         out = dot_t(feats[at_block(kb), :], query) * scale
         if diagonal:
             out = jnp.where(key_row <= query_col, out, NEG)
-        return out.reshape(deep)
+        return [out[c * CH : (c + 1) * CH].reshape(deep) for c in range(BLK // CH)]
 
     def student_tile(kb, qb, query, state, diagonal):
         top, total = state
         t = tile_of(kb, qb)
-        logit = logits(s_all, kb, query, scale_s, diagonal)
-        new = jnp.maximum(top, jnp.max(logit, axis=0))
-        weight = jnp.exp2(logit - new)
-        log_s[t] = logit.reshape(BLK, BLK)
-        w_s[t] = weight.reshape(BLK, BLK)
-        top_s[t] = new
-        return new, total * jnp.exp2(top - new) + jnp.sum(weight, axis=0)
+        for c, logit in enumerate(logits(s_all, kb, query, scale_s, diagonal)):
+            new = jnp.maximum(top, jnp.max(logit, axis=0))
+            weight = jnp.exp2(logit - new)
+            log_s[t, c * CH : (c + 1) * CH, :] = logit.reshape(CH, BLK)
+            w_s[t, c * CH : (c + 1) * CH, :] = weight.reshape(CH, BLK)
+            top_s[t, c] = new
+            total = total * jnp.exp2(top - new) + jnp.sum(weight, axis=0)
+            top = new
+        return top, total
 
     def teacher_tile(kb, qb, query, state, diagonal):
         top, total, cross = state
         t = tile_of(kb, qb)
-        logit = logits(t_all, kb, query, scale_t, diagonal)
-        new = jnp.maximum(top, jnp.max(logit, axis=0))
-        weight = jnp.exp2(logit - new)
-        w_t[t] = weight.reshape(BLK, BLK)
-        top_t[t] = new
-        again = jnp.exp2(top - new)
-        gap = logit - log_s[t].reshape(deep)
-        return (
-            new,
-            total * again + jnp.sum(weight, axis=0),
-            cross * again + jnp.sum(weight * gap, axis=0),
-        )
+        for c, logit in enumerate(logits(t_all, kb, query, scale_t, diagonal)):
+            new = jnp.maximum(top, jnp.max(logit, axis=0))
+            weight = jnp.exp2(logit - new)
+            w_t[t, c * CH : (c + 1) * CH, :] = weight.reshape(CH, BLK)
+            top_t[t, c] = new
+            again = jnp.exp2(top - new)
+            gap = logit - log_s[t, c * CH : (c + 1) * CH, :].reshape(deep)
+            total = total * again + jnp.sum(weight, axis=0)
+            cross = cross * again + jnp.sum(weight * gap, axis=0)
+            top = new
+        return top, total, cross
 
     def sweep(tile, feats, wq, fresh):
         qa, qb = 2 * wq, 2 * wq + 1
@@ -227,7 +229,6 @@
 
         def turn(b, c):
             s_turn[:, at_block(b)] = s_all[at_block(b), :].T
-            col[at_block(b), :] = jnp.zeros((BLK, HD), F32)
             return c
 
         lax.fori_loop(0, 2 * wide, turn, 0)
@@ -241,9 +242,8 @@
 
         loop(wide, student_block, 0)
 
-        await_bytes(t_all, t_recv)
-
         def teacher_block(wq, loss_row):
+            await_bytes(t_all.at[pl.ds(2 * wq * BLK, 2 * BLK), :], t_recv.at[wq])
             for q, (top, total, cross) in sweep(teacher_tile, t_all, wq, (low, zero, zero)):
                 peak = jnp.max(top, axis=0, keepdims=True)
                 again = jnp.exp2(top - peak)
@@ -268,40 +268,30 @@
 
         def diff(kb, q):
             t = tile_of(kb, q)
-            ours = w_s[t].reshape(deep) * jnp.exp2(top_s[t] - lse_s[q])
-            theirs = w_t[t].reshape(deep) * jnp.exp2(top_t[t] - lse_t[q])
-            return (ours - theirs).reshape(BLK, BLK).astype(BF16)
-
-        def add(kb, q, query, row):
-            d = diff(kb, q)
-            col[at_block(kb), :] += jnp.dot(d, query, preferred_element_type=F32)
-            return row + jnp.dot(s_turn[:, at_block(kb)], d, preferred_element_type=F32)
-
-        def grad_block(step, c):
-            wq = wide - 1 - step
-            qa, qb = 2 * wq, 2 * wq + 1
-            query_a, query_b = s_all[at_block(qa), :], s_all[at_block(qb), :]
-
-            def full(i, c):
-                row_a, row_b = c
-                for kb in (2 * i, 2 * i + 1):
-                    row_a = add(kb, qa, query_a, row_a)
-                    row_b = add(kb, qb, query_b, row_b)
-                return row_a, row_b
-
-            none = jnp.zeros((HD, BLK), F32)
-            row_a, row_b = none, none
-            for i in range(wq):
-                row_a, row_b = full(i, (row_a, row_b))
-            row_a = add(qa, qa, query_a, row_a)
-            row_b = add(qa, qb, query_b, row_b)
-            row_b = add(qb, qb, query_b, row_b)
-            for q, row in ((qa, row_a), (qb, row_b)):
-                block = (col[at_block(q), :] + row.T) * (1.0 / math.sqrt(HD))
-                back[at_block(q), :] = block.astype(BF16)
-            for j in range(per_blk):
-                s = wq * per_blk + j
-                src = back.at[pl.ds(pl.multiple_of(s * rows, rows), rows), :]
+            parts = []
+            for c in range(BLK // CH):
+                ours = w_s[t, c * CH : (c + 1) * CH, :].reshape(deep) * jnp.exp2(top_s[t, c] - lse_s[q])
+                theirs = w_t[t, c * CH : (c + 1) * CH, :].reshape(deep) * jnp.exp2(top_t[t, c] - lse_t[q])
+                parts.append((ours - theirs).reshape(CH, BLK).astype(BF16))
+            return jnp.concatenate(parts, axis=0)
+
+        for kb in range(2 * wide):
+            keys_turned = s_turn[:, at_block(kb)]
+            col = jnp.zeros((BLK, HD), F32)
+            for q in range(kb, 2 * wide):
+                d = diff(kb, q)
+                col = col + jnp.dot(d, s_all[at_block(q), :], preferred_element_type=F32)
+                row = jnp.dot(keys_turned, d, preferred_element_type=F32)
+                if kb > 0:
+                    row = row + rows_turned[:, at_block(q)]
+                if q > kb:
+                    rows_turned[:, at_block(q)] = row
+                else:
+                    last = row
+            back[at_block(kb), :] = ((col + last.T) * (1.0 / math.sqrt(HD))).astype(BF16)
+            for j in range(BLK // rows):
+                s = kb * (BLK // rows) + j
+                src = back.at[pl.ds(s * rows, rows), :]
                 dst = grads.at[my_p, :, pl.ds(pl.multiple_of(my_rl * HD, HD), HD)]
 
                 @pl.when(s != me_s)
@@ -312,9 +302,6 @@
                 def _():
                     pltpu.make_async_copy(src, dst, g_recv).start()
 
-            return c
-
-        loop(wide, grad_block, 0)
         await_bytes(l_seq.at[pl.ds(0, 3 * rels - 1)], l_recv.at[0])
 
     @pl.when(jnp.logical_not(active))
@@ -378,7 +365,7 @@
             ],
             out_specs=(
                 pl.BlockSpec(memory_space=pltpu.SMEM),
-                pl.BlockSpec(memory_space=pltpu.HBM),
+                pl.BlockSpec(memory_space=pl.ANY),
             ),
             scratch_shapes=[pltpu.SMEM(table.shape, jnp.int32)]
             + [pltpu.VMEM((nh, sub, width), BF16)] * 3
@@ -391,27 +378,27 @@
                 pltpu.VMEM((tiles, BLK, BLK), F32),
                 pltpu.VMEM((tiles, BLK, BLK), F32),
                 pltpu.VMEM((tiles, BLK, BLK), F32),
-                pltpu.VMEM((tiles, 8, BLK), F32),
-                pltpu.VMEM((tiles, 8, BLK), F32),
+                pltpu.VMEM((tiles, BLK // CH, 8, BLK), F32),
+                pltpu.VMEM((tiles, BLK // CH, 8, BLK), F32),
                 pltpu.VMEM((blocks, 8, BLK), F32),
                 pltpu.VMEM((blocks, 8, BLK), F32),
-                pltpu.VMEM((tokens, HD), F32),
+                pltpu.VMEM((HD, tokens), F32),
                 pltpu.VMEM((tokens, HD), BF16),
                 pltpu.VMEM((8, HD), F32),
                 pltpu.VMEM((ns, 8, HD), F32),
                 pltpu.VMEM((nh, 8, HD), F32),
-                dma, dma, dma((3,)), dma, dma, dma, dma, dma, dma, dma((2,)), dma((2,)),
+                dma, dma, dma((3,)), dma, dma, dma, dma((blocks // 2,)), dma, dma, dma((2,)), dma((2,)),
                 pltpu.SemaphoreType.REGULAR,
             ],
             compiler_params=pltpu.CompilerParams(
-                has_side_effects=True, collective_id=0, vmem_limit_bytes=60 * 1024 * 1024
+                has_side_effects=True, collective_id=0, vmem_limit_bytes=48 * 1024 * 1024
             ),
             cost_estimate=pl.CostEstimate(
                 flops=tokens * tokens * 1280, bytes_accessed=4 * 1024 * 1024,
                 transcendentals=tokens * tokens,
             ),
             name="relations",
-        )(table, jnp.transpose(teacher, (1, 0, 2)), jnp.transpose(student, (1, 0, 2)))
+        )(*[pltpu.with_memory_space_constraint(x, pltpu.HBM) for x in (table, jnp.transpose(teacher, (1, 0, 2)), jnp.transpose(student, (1, 0, 2)))])
         return loss.reshape(()), jnp.transpose(grads, (1, 0, 2))
 
     return jax.shard_map(

time: 53.1 us -> 50.6 us (0.953)
  Pallas kernels: 48.5 us -> 47.1 us
  local copies, waits for them, and re-layouts: 1.77 us -> 0.75 us
    pallas_call x1, Pallas kernels: 48.5 us -> 47.1 us  [body(): pl.pallas_call(functools.partial(kernel, ns, nh), out_shape=(jax.ShapeDty...]
    unnamed x1, local copies, waits for them, and re-layouts: 1.77 us -> 0.75 us
where the time goes in v3:
time: 50.6 us; the launch traced here: 50.2 us
  Pallas kernels  47.1 us (93%)
  between operations  2.33 us (5%)
  local copies, waits for them, and re-layouts  0.75 us (1%)
    pallas_call x1, Pallas kernels, body(): pl.pallas_call(functools.partial(kernel, ns, nh), out_shape=(jax.ShapeDty...  47.1 us

profile of v3, /device:TPU:1, one launch (start us, length us, event | category | flops | bytes accessed | tf_op | source)
XLA Modules:
  0.0 50.2 jit_solution(6543132448685147627)
XLA Ops:
  0.6 47.1 %relations.1 = (f32[1]{0:T(128)}, bf16[3,128,512]{2,1,0:T(8,128)(2,1)S(1)}) custom-call(s32[64]{0:T(128)} %table_hbm.1, bf16[3,128,1024]{2,1,0:T(8,128)(2,1)} %bitcast.5, bf16[3,128,512]{2,1,0:T(8,128)(2,1)} %bitcast.6), custom_call_target="tpu_custom_call" | custom-call | flops 5368709120 | bytes 4194304 | tf_op jit(solution)/shard_map/relations/pallas_call | solution.py:355
  48.3 0.7 %copy.8 = bf16[128,3,512]{2,0,1:T(8,128)(2,1)} copy(bf16[128,3,512]{2,0,1:T(8,128)(2,1)S(1)} %bitcast.4) | data formatting | bytes 786432

commit v4 on v3

--- a/solution.py
+++ b/solution.py
@@ -14,6 +14,7 @@
 CH = 256
 NEG = -1e30
 MESH = pl.DeviceIdType.MESH
+FAR_FIRST = [(2, 1), (1, 1), (3, 1), (2, 0), (0, 1), (1, 0), (3, 0)]
 F32 = jnp.float32
 BF16 = jnp.bfloat16
 LOG2E = math.log2(math.e)
@@ -42,7 +43,7 @@
     got0, got1, got2, flat0, flat1, flat2, stage0, stage1, stage2,
     t_all, s_all, s_turn, log_s, w_s, w_t, top_s, top_t, lse_s, lse_t, rows_turned, back,
     l_mine, l_seq, l_head,
-    tab_sem, p1_send, p1_recv, s_send, s_recv, p2_send, t_recv, g_send, g_recv, l_send, l_recv, all_in,
+    tab_sem, p1_send, p1_recv, s_send, s_recv, p2_send, t_recv, g_send, g_recv, l_send, l_recv, all_in, t_near, s_near, pre_sem,
 ):
     rows = teacher.shape[1]
     width = teacher.shape[2]
@@ -85,11 +86,19 @@
     greet(barrier, True)
     table_copy = pltpu.make_async_copy(table_hbm, table, tab_sem)
     table_copy.start()
+    pre_t = pltpu.make_async_copy(teacher, t_near, pre_sem.at[0])
+    pre_s = pltpu.make_async_copy(student, s_near, pre_sem.at[1])
+    pre_t.start()
+    pre_s.start()
     pl.semaphore_wait(barrier, ns + nh - 2)
+    pre_t.wait()
+    pre_s.wait()
+    teacher, student = t_near, s_near
 
     for p in range(3):
         for step in range(1, nh):
-            g = lax.rem(me_g + step, nh)
+            dy, dx = FAR_FIRST[step - 1] if nh == 8 else (step // 2, step % 2)
+            g = lax.rem(me_g // 2 + dy, nh // 2) * 2 + lax.rem(me_g + dx, 2)
             send(
                 teacher.at[p, pl.ds(g * sub, sub), :], got[p].at[me_g],
                 p1_send, p1_recv.at[p], me_s, g,
@@ -255,16 +264,20 @@
             return loss_row
 
         loss_row = loop(wide, teacher_block, zero)
-        mine = jnp.full((8, HD), jnp.sum(loss_row) * 0.125, F32)
+        mine = loss_row[:, :HD] + loss_row[:, HD:]
         l_mine[...] = mine
         l_seq[me_s] = mine
 
         def loss_out(i, c):
-            s = lax.rem(me_s + 1 + i, ns)
-            send(l_mine, l_seq.at[me_s], l_send.at[0], l_recv.at[0], s, me_g)
+            s = 4 * (i // 4) + lax.rem(me_s + i, 4)
+
+            @pl.when(s != me_s)
+            def _():
+                send(l_mine, l_seq.at[me_s], l_send.at[0], l_recv.at[0], s, me_g)
+
             return c
 
-        lax.fori_loop(0, ns - 1, loss_out, 0)
+        lax.fori_loop(0, ns, loss_out, 0)
 
         def diff(kb, q):
             t = tile_of(kb, q)
@@ -320,7 +333,7 @@
     total = l_head[0]
     for g in range(1, nh):
         total = total + l_head[g]
-    loss[0] = total[0, 0] * (1.0 / (LOG2E * 3.0 * rel_all * tokens))
+    loss[0] = jnp.sum(total) * (0.125 / (LOG2E * 3.0 * rel_all * tokens))
 
     await_bytes(teacher.at[:, pl.ds(0, rows - sub), :], p1_send)
 
@@ -389,6 +402,9 @@
                 pltpu.VMEM((nh, 8, HD), F32),
                 dma, dma, dma((3,)), dma, dma, dma, dma((blocks // 2,)), dma, dma, dma((2,)), dma((2,)),
                 pltpu.SemaphoreType.REGULAR,
+                pltpu.VMEM((3, rows, width), BF16),
+                pltpu.VMEM((3, rows, swidth), BF16),
+                dma((2,)),
             ],
             compiler_params=pltpu.CompilerParams(
                 has_side_effects=True, collective_id=0, vmem_limit_bytes=48 * 1024 * 1024

time: 50.6 us -> 50.1 us (level)
  no operation moved by 1% of the time
where the time goes in v4:
time: 50.1 us; the launch traced here: 50 us
  Pallas kernels  46.9 us (94%)
  between operations  2.33 us (5%)
  local copies, waits for them, and re-layouts  0.75 us (1%)
    pallas_call x1, Pallas kernels, body(): pl.pallas_call(functools.partial(kernel, ns, nh), out_shape=(jax.ShapeDty...  46.9 us

profile of v4, /device:TPU:1, one launch (start us, length us, event | category | flops | bytes accessed | tf_op | source)
XLA Modules:
  0.0 50.0 jit_solution(4014472521128821243)
XLA Ops:
  0.6 46.9 %relations.1 = (f32[1]{0:T(128)}, bf16[3,128,512]{2,1,0:T(8,128)(2,1)S(1)}) custom-call(s32[64]{0:T(128)} %table_hbm.1, bf16[3,128,1024]{2,1,0:T(8,128)(2,1)} %bitcast.5, bf16[3,128,512]{2,1,0:T(8,128)(2,1)} %bitcast.6), custom_call_target="tpu_custom_call" | custom-call | flops 5368709120 | bytes 4194304 | tf_op jit(solution)/shard_map/relations/pallas_call | solution.py:368
  48.1 0.7 %copy.8 = bf16[128,3,512]{2,0,1:T(8,128)(2,1)} copy(bf16[128,3,512]{2,0,1:T(8,128)(2,1)S(1)} %bitcast.4) | data formatting | bytes 786432

commit v5 on v4

--- a/solution.py
+++ b/solution.py
@@ -14,6 +14,7 @@
 CH = 256
 NEG = -1e30
 MESH = pl.DeviceIdType.MESH
+SEQ_FAR = [(z, k) for z in (2, 1, 3, 0) for k in (2, 3, 1, 0) if z or k]
 FAR_FIRST = [(2, 1), (1, 1), (3, 1), (2, 0), (0, 1), (1, 0), (3, 0)]
 F32 = jnp.float32
 BF16 = jnp.bfloat16
@@ -72,15 +73,14 @@
     barrier = pltpu.get_barrier_semaphore()
 
     def greet(sem, along_seq):
-        def one(i, c):
+        for step in range(1, ns if along_seq else nh):
             if along_seq:
-                to = (lax.rem(me_s + i, ns), me_g)
+                dz, dk = SEQ_FAR[step - 1]
+                to = (lax.rem(me_s // 4 + dz, 4) * 4 + lax.rem(me_s + dk, 4), me_g)
             else:
-                to = (me_s, lax.rem(me_g + i, nh))
+                dy, dx = FAR_FIRST[step - 1]
+                to = (me_s, lax.rem(me_g // 2 + dy, nh // 2) * 2 + lax.rem(me_g + dx, 2))
             pl.semaphore_signal(sem, inc=1, device_id=to, device_id_type=MESH)
-            return c
-
-        lax.fori_loop(1, ns if along_seq else nh, one, 0)
 
     greet(barrier, False)
     greet(barrier, True)
@@ -92,22 +92,7 @@
     pre_s.start()
     pl.semaphore_wait(barrier, ns + nh - 2)
     pre_t.wait()
-    pre_s.wait()
     teacher, student = t_near, s_near
-
-    for p in range(3):
-        for step in range(1, nh):
-            dy, dx = FAR_FIRST[step - 1] if nh == 8 else (step // 2, step % 2)
-            g = lax.rem(me_g // 2 + dy, nh // 2) * 2 + lax.rem(me_g + dx, 2)
-            send(
-                teacher.at[p, pl.ds(g * sub, sub), :], got[p].at[me_g],
-                p1_send, p1_recv.at[p], me_s, g,
-            )
-        pltpu.make_async_copy(
-            teacher.at[p, pl.ds(me_g * sub, sub), :], got[p].at[me_g], p1_recv.at[p]
-        ).start()
-
-    greet(all_in, False)
 
     def student_out(i, c):
         q = lax.rem(i + me_s, 3 * rels)
@@ -127,7 +112,25 @@
 
         return c
 
-    lax.fori_loop(0, 3 * rels, student_out, 0)
+    for p in range(3):
+        for step in range(1, nh):
+            dy, dx = FAR_FIRST[step - 1]
+            g = lax.rem(me_g // 2 + dy, nh // 2) * 2 + lax.rem(me_g + dx, 2)
+            send(
+                teacher.at[p, pl.ds(g * sub, sub), :], got[p].at[me_g],
+                p1_send, p1_recv.at[p], me_s, g,
+            )
+            if p == 2:
+                if step == 1:
+                    pre_s.wait()
+                student_out(step - 1, 0)
+        pltpu.make_async_copy(
+            teacher.at[p, pl.ds(me_g * sub, sub), :], got[p].at[me_g], p1_recv.at[p]
+        ).start()
+
+    greet(all_in, False)
+
+    lax.fori_loop(nh - 1, 3 * rels, student_out, 0)
     table_copy.wait()
     pl.semaphore_wait(all_in, nh - 1)
 
@@ -327,7 +330,9 @@
             group = group + l_seq[s]
     l_head[me_g] = group
     for step in range(1, nh):
-        send(l_head.at[me_g], l_head.at[me_g], l_send.at[1], l_recv.at[1], me_s, lax.rem(me_g + step, nh))
+        dy, dx = FAR_FIRST[step - 1]
+        g = lax.rem(me_g // 2 + dy, nh // 2) * 2 + lax.rem(me_g + dx, 2)
+        send(l_head.at[me_g], l_head.at[me_g], l_send.at[1], l_recv.at[1], me_s, g)
     await_bytes(grads, g_recv)
     await_bytes(l_head.at[pl.ds(0, nh - 1)], l_recv.at[1])
     total = l_head[0]

time: 50.1 us -> 49.9 us (level)
  no operation moved by 1% of the time
where the time goes in v5:
time: 49.9 us; the launch traced here: 49.8 us
  Pallas kernels  46.7 us (94%)
  between operations  2.33 us (5%)
  local copies, waits for them, and re-layouts  0.75 us (2%)
    pallas_call x1, Pallas kernels, body(): pl.pallas_call(functools.partial(kernel, ns, nh), out_shape=(jax.ShapeDty...  46.7 us

profile of v5, /device:TPU:1, one launch (start us, length us, event | category | flops | bytes accessed | tf_op | source)
XLA Modules:
  0.0 49.8 jit_solution(14839845512039471596)
XLA Ops:
  0.6 46.7 %relations.1 = (f32[1]{0:T(128)}, bf16[3,128,512]{2,1,0:T(8,128)(2,1)S(1)}) custom-call(s32[64]{0:T(128)} %table_hbm.1, bf16[3,128,1024]{2,1,0:T(8,128)(2,1)} %bitcast.5, bf16[3,128,512]{2,1,0:T(8,128)(2,1)} %bitcast.6), custom_call_target="tpu_custom_call" | custom-call | flops 5368709120 | bytes 4194304 | tf_op jit(solution)/shard_map/relations/pallas_call | solution.py:373
  47.9 0.7 %copy.8 = bf16[128,3,512]{2,0,1:T(8,128)(2,1)} copy(bf16[128,3,512]{2,0,1:T(8,128)(2,1)S(1)} %bitcast.4) | data formatting | bytes 786432

commit v6 on v4

--- a/solution.py
+++ b/solution.py
@@ -232,6 +232,20 @@
     low = jnp.full((8, BLK), NEG, F32)
     zero = jnp.zeros((8, BLK), F32)
 
+    def give_back(kb):
+        for j in range(BLK // rows):
+            s = kb * (BLK // rows) + j
+            src = back.at[pl.ds(s * rows, rows), :]
+            dst = grads.at[my_p, :, pl.ds(pl.multiple_of(my_rl * HD, HD), HD)]
+
+            @pl.when(s != me_s)
+            def _():
+                send(src, dst, g_send, g_recv, s, me_g)
+
+            @pl.when(s == me_s)
+            def _():
+                pltpu.make_async_copy(src, dst, g_recv).start()
+
     @pl.when(active)
     def _():
         await_bytes(s_all, s_recv)
@@ -302,18 +316,8 @@
                 else:
                     last = row
             back[at_block(kb), :] = ((col + last.T) * (1.0 / math.sqrt(HD))).astype(BF16)
-            for j in range(BLK // rows):
-                s = kb * (BLK // rows) + j
-                src = back.at[pl.ds(s * rows, rows), :]
-                dst = grads.at[my_p, :, pl.ds(pl.multiple_of(my_rl * HD, HD), HD)]
-
-                @pl.when(s != me_s)
-                def _():
-                    send(src, dst, g_send, g_recv, s, me_g)
-
-                @pl.when(s == me_s)
-                def _():
-                    pltpu.make_async_copy(src, dst, g_recv).start()
+            if kb < 2 * wide - 2:
+                give_back(kb)
 
         await_bytes(l_seq.at[pl.ds(0, 3 * rels - 1)], l_recv.at[0])
 
@@ -328,6 +332,11 @@
     l_head[me_g] = group
     for step in range(1, nh):
         send(l_head.at[me_g], l_head.at[me_g], l_send.at[1], l_recv.at[1], me_s, lax.rem(me_g + step, nh))
+    @pl.when(active)
+    def _():
+        for kb in range(2 * wide - 2, 2 * wide):
+            give_back(kb)
+
     await_bytes(grads, g_recv)
     await_bytes(l_head.at[pl.ds(0, nh - 1)], l_recv.at[1])
     total = l_head[0]

time: 50.1 us -> 52.3 us (1.044)
  Pallas kernels: 46.9 us -> 49.1 us
    pallas_call x1, Pallas kernels: 46.9 us -> 49.1 us  [body(): pl.pallas_call(functools.partial(kernel, ns, nh), out_shape=(jax.ShapeDty...]
where the time goes in v6:
time: 52.3 us; the launch traced here: 52.2 us
  Pallas kernels  49.1 us (94%)
  between operations  2.33 us (4%)
  local copies, waits for them, and re-layouts  0.75 us (1%)
    pallas_call x1, Pallas kernels, body(): pl.pallas_call(functools.partial(kernel, ns, nh), out_shape=(jax.ShapeDty...  49.1 us

profile of v6, /device:TPU:1, one launch (start us, length us, event | category | flops | bytes accessed | tf_op | source)
XLA Modules:
  0.0 52.2 jit_solution(9821968230214679965)
XLA Ops:
  0.6 49.1 %relations.1 = (f32[1]{0:T(128)}, bf16[3,128,512]{2,1,0:T(8,128)(2,1)S(1)}) custom-call(s32[64]{0:T(128)} %table_hbm.1, bf16[3,128,1024]{2,1,0:T(8,128)(2,1)} %bitcast.5, bf16[3,128,512]{2,1,0:T(8,128)(2,1)} %bitcast.6), custom_call_target="tpu_custom_call" | custom-call | flops 5368709120 | bytes 4194304 | tf_op jit(solution)/shard_map/relations/pallas_call | solution.py:377
  50.3 0.7 %copy.8 = bf16[128,3,512]{2,0,1:T(8,128)(2,1)} copy(bf16[128,3,512]{2,0,1:T(8,128)(2,1)S(1)} %bitcast.4) | data formatting | bytes 786432
